TPU v7x, 512 devices: a whole 4x4x16 slice. The times are simulated.
512 devices in a mesh: replica: 16 (over z_hi, x), tensor: 32 (over y, z_lo, core).
Axes of the slice: x: 4, y: 4, z: 16 (z_hi: 4, z_lo: 4; z = z_hi * 4 + z_lo), core: 2. Of those that a mesh axis runs over, the one named last changes fastest.
Arguments:
- attn_out: bfloat16 [16, 1024, 4096], P('replica', None, 'tensor'), may hold values from -6 to 6
- resid_in: bfloat16 [16, 1024, 2048], P('replica', 'tensor')
- out_weight: bfloat16 [16, 4096, 2048], P('replica', 'tensor'), may hold values from -6 to 6
- velocity: bfloat16 [16, 4096, 2048], P('replica', 'tensor'), may hold values from -6 to 6
- norm_gain: bfloat16 [2048], replicated, may hold values from 0.099609375 to 1.8984375
- grad_normed: bfloat16 [16, 1024, 2048], P('replica', 'tensor'), may hold values from -6 to 6
- grad_resid: bfloat16 [16, 1024, 2048], P('replica', 'tensor'), may hold values from -6 to 6
- step_count: int32 [1], replicated, may hold values from 0 to 1048575
Outputs:
- stream: bfloat16 [16, 1024, 2048], P('replica', 'tensor')
- grad_attn: bfloat16 [16, 1024, 4096], P('replica', None, 'tensor')
- new_weight: bfloat16 [16, 4096, 2048], P('replica', 'tensor')
- new_velocity: bfloat16 [16, 4096, 2048], P('replica', 'tensor')
All inputs are finite; a program needn't handle non-finite values.
Results may differ from a plain program's by a relative error of at most 0.015.
Values may be sent and summed in bfloat16 or wider, within the bound.
A program may use at most 64 MiB of HBM per device.

v0:
```python
from functools import partial

import jax
import jax.numpy as jnp
from jax import lax
from jax.sharding import PartitionSpec as P

D = 2048
INNER = 4096


norm_eps = 1e-05
decay_coef = 0.9
step_span = 1048576.0


def as_sent(array):

    def short(part):
        return part.astype(jnp.bfloat16) if part.dtype == jnp.float32 else part

    return jax.tree.map(short, array)


def from_partner(block, axis, bit):
    count = lax.axis_size(axis)
    route = []
    for low in range(count):
        high = low | 1 << bit
        if high != low and high < count:
            route += [(low, high), (high, low)]
    return lax.ppermute(block, axis, route)


def plan_rate(step_value):
    phase = step_value.astype(jnp.float32) * (jnp.pi / step_span)
    return 0.02 + 0.04 * (1.0 + jnp.cos(phase))


def trade_updated(state_pair, bit_number):
    return jax.tree.map(
        lambda part, own: part.astype(own.dtype),
        from_partner(as_sent(state_pair), "replica", bit_number),
        state_pair,
    )


def per_device(
    attn_out, resid_in, out_weight, velocity, norm_gain, grad_normed, grad_resid, step_count
):
    heads_out = attn_out[0]
    weight = out_weight[0]
    own_velocity = velocity[0]
    inv_width = INNER ** (-0.5)
    bit_count = lax.axis_size("replica").bit_length() - 1
    peer_bit = step_count[0] % bit_count
    learn_rate = plan_rate(step_count[0])
    row_block = heads_out
    projected = lax.psum_scatter(
        (jnp.dot(row_block, weight, preferred_element_type=jnp.float32) * inv_width).astype(
            jnp.bfloat16
        ),
        "tensor",
        scatter_dimension=0,
        tiled=True,
    ).astype(jnp.float32)
    stream = (resid_in[0].astype(jnp.float32) + projected).astype(jnp.bfloat16)
    stream32 = stream.astype(jnp.float32)
    inv_rms = lax.rsqrt(jnp.mean(stream32 * stream32, axis=-1, keepdims=True) + norm_eps)
    upstream = norm_gain.astype(jnp.float32) * grad_normed[0].astype(jnp.float32)
    inner_sum = jnp.sum(upstream * stream32, axis=-1, keepdims=True)
    dstream = (
        grad_resid[0].astype(jnp.float32)
        + inv_rms * upstream
        - stream32 * inv_rms**3 * inner_sum / D
    )
    dstream = dstream.astype(jnp.bfloat16)
    shard_rows = lax.all_gather(dstream, "tensor", axis=0, tiled=True)
    row_block = heads_out
    weight_total = jnp.einsum(
        "tg,td->gd", row_block, shard_rows, preferred_element_type=jnp.float32
    )
    back_rows = jnp.einsum("td,gd->tg", shard_rows, weight, preferred_element_type=jnp.float32)
    input_total = back_rows
    weight_total, input_total = (weight_total, input_total)
    grad_attn = (input_total * inv_width).astype(jnp.bfloat16)
    weight_grad = (weight_total * inv_width).astype(jnp.bfloat16)
    velocity_local = decay_coef * own_velocity.astype(jnp.float32) + weight_grad.astype(jnp.float32)
    weight_local = weight.astype(jnp.float32) - learn_rate * velocity_local
    updated_branches = [
        partial(trade_updated, bit_number=bit_number) for bit_number in range(bit_count)
    ]
    peer_weight_local, peer_velocity_local = lax.switch(
        peer_bit, updated_branches, (weight_local, velocity_local)
    )
    new_velocity = (0.5 * (velocity_local + peer_velocity_local)).astype(jnp.bfloat16)
    new_weight = (0.5 * (weight_local + peer_weight_local)).astype(jnp.bfloat16)
    return (stream[None], grad_attn[None], new_weight[None], new_velocity[None])


def solution(mesh):
    placed = (
        P("replica", None, "tensor"),
        P("replica", "tensor", None),
        P("replica", "tensor", None),
        P("replica", "tensor", None),
        P(),
        P("replica", "tensor", None),
        P("replica", "tensor", None),
        P(),
    )
    return jax.shard_map(
        per_device,
        mesh=mesh,
        in_specs=placed,
        out_specs=(
            P("replica", "tensor", None),
            P("replica", None, "tensor"),
            P("replica", "tensor", None),
            P("replica", "tensor", None),
        ),
        check_vma=False,
    )
```

profile of v0, /device:TPU:1, one launch (start us, length us, event | category | flops | bytes accessed | tf_op | source)
XLA Modules:
  0.0 294.5 jit_solution(11138269662916701953)
XLA Ops:
  7.2 0.0 copy-start
  7.2 0.0 copy-start.8
  7.2 0.0 copy-start.4
  7.2 0.0 copy-start.7
  7.2 0.0 reduce-scatter.2.cloned.1.call-start
  7.3 0.9 copy-done
  8.1 4.2 %multiply_convert_fusion = bf16[1024,2048]{1,0:T(8,128)(2,1)} fusion(bf16[1,128,2048]{2,1,0:T(8,128)(2,1)} %param.14, bf16[1,1024,128]{2,1,0:T(8,128)(2,1)S(1)} %copy-done), kind=kOutput, calls=%fused_computation | convolution fusion | flops 541065216 | bytes 4980736 | tf_op jit(solution)/shard_map/dot_general | solution.py:60
  12.4 0.0 copy-start.6
  12.4 0.0 copy-start.1
  12.4 0.0 copy-start.3
  12.4 0.0 reduce-scatter.2.cloned.1.call-update
  12.4 0.0 all-gather.2.cloned.1.call-start
  12.4 0.0 copy-done.8
  12.5 159.0 %reduce-scatter.2.cloned.1.call-done = bf16[32,2048]{1,0:T(8,128)(2,1)} async-done(((bf16[1024,2048]{1,0:T(8,128)(2,1)}), bf16[32,2048]{1,0:T(8,128)(2,1)}) %reduce-scatter.2.cloned.1.call-update) | async-done | bytes 131088 | tf_op jit(solution)/shard_map/reduce_scatter | solution.py:59
  171.5 0.0 copy-done.4
  171.5 0.0 copy-done.7
  171.5 1.1 fusion.14
  172.6 0.0 copy-start.5
  172.6 0.0 copy-done.6
  172.6 0.8 fusion.18
  173.4 0.0 all-gather.2.cloned.1.call-update
  174.1 0.0 copy-done.1
  174.1 0.3 copy.12
  174.5 0.0 copy-done.3
  174.5 0.3 copy.13
  174.8 68.8 %all-gather.2.cloned.1.call-done = bf16[1024,2048]{1,0:T(8,128)(2,1)} async-done(((bf16[32,2048]{1,0:T(8,128)(2,1)}), bf16[1024,2048]{1,0:T(8,128)(2,1)}) %all-gather.2.cloned.1.call-update) | async-done | bytes 4194320 | tf_op jit(solution)/shard_map/all_gather | solution.py:78
  243.6 3.5 %multiply_subtract_fusion = (f32[128,2048]{0,1:T(8,128)S(1)}, f32[128,2048]{0,1:T(8,128)S(1)}) fusion(bf16[1,128,2048]{1,2,0:T(8,128)(2,1)S(1)} %copy.12, f32[]{:T(128)S(6)} %add_shard_map.7, bf16[1024,2048]{1,0:T(8,128)(2,1)} %all-gather.2.cloned.1.call-done, bf16[1,1024,128]{2,1,0:T(8,128)(2,1)S(1)} %copy-done, bf16[1,128,2048]{1,2,0:T(8,128)(2,1)S(1)} %copy.13), kind=kOutput, calls=%fused_computation.15 | convolution fusion | flops 539230208 | bytes 7602180 | tf_op jit(solution)/shard_map/tg,td->gd/dot_general | solution.py:80
  247.0 0.0 copy-done.5
  247.1 26.7 %conditional.4 = (bf16[128,2048]{1,0:T(8,128)(2,1)}, bf16[128,2048]{1,0:T(8,128)(2,1)}) conditional(s32[]{:T(128)} %clamp.3, (f32[128,2048]{0,1:T(8,128)S(1)}, f32[128,2048]{0,1:T(8,128)S(1)}) %multiply_subtract_fusion, (f32[128,2048]{0,1:T(8,128)S(1)}, f32[128,2048]{0,1:T(8,128)S(1)}) %multiply_subtract_fusion, ...), branch_computations={%region_3.4_spmd, %region_4.5_spmd, %region_5.6_spmd, %region_6.7_... | conditional | bytes 7340128
  247.1 0.2 copy.14
  247.3 3.1 %collective-permute-start = (bf16[128,2048]{1,0:T(8,128)(2,1)S(1)}, bf16[128,2048]{1,0:T(8,128)(2,1)}, u32[]{:S(2)}, u32[]{:S(2)}) collective-permute-start(bf16[128,2048]{1,0:T(8,128)(2,1)S(1)} %copy.14), channel_id=1, source_target_pairs={{0,32},{32,0},{64,96},{96,64},{128,160},{160,128},{192,224},{224,1... | collective-permute-start | bytes 1572872 | tf_op jit(solution)/shard_map/cond/branch_0_fun/ppermute | solution.py:32
  250.4 0.2 copy.15
  250.6 2.2 collective-permute-start.1
  252.8 9.7 %collective-permute-done = bf16[128,2048]{1,0:T(8,128)(2,1)} collective-permute-done((bf16[128,2048]{1,0:T(8,128)(2,1)S(1)}, bf16[128,2048]{1,0:T(8,128)(2,1)}, u32[]{:S(2)}, u32[]{:S(2)}) %collective-permute-start) | collective-permute-done | bytes 524320 | tf_op jit(solution)/shard_map/cond/branch_0_fun/ppermute | solution.py:32
  262.5 11.2 %collective-permute-done.1 = bf16[128,2048]{1,0:T(8,128)(2,1)} collective-permute-done((bf16[128,2048]{1,0:T(8,128)(2,1)S(1)}, bf16[128,2048]{1,0:T(8,128)(2,1)}, u32[]{:S(2)}, u32[]{:S(2)}) %collective-permute-start.1) | collective-permute-done | bytes 524320 | tf_op jit(solution)/shard_map/cond/branch_0_fun/ppermute | solution.py:32
  273.8 0.0 copy-start.2
  273.8 1.4 copy.23
  275.1 2.0 copy.22
  277.2 2.3 fusion.10
  279.5 2.0 copy.24
  281.5 2.0 copy.25
  283.6 0.0 copy-done.2
  283.6 4.1 %fusion.5 = bf16[1,1024,128]{2,1,0:T(8,128)(2,1)} fusion(bf16[1024,2048]{1,0:T(8,128)(2,1)} %all-gather.2.cloned.1.call-done, bf16[1,128,2048]{2,1,0:T(8,128)(2,1)S(1)} %copy-done.2), kind=kOutput, calls=%fused_computation.8 | convolution fusion | flops 537133056 | bytes 4980736 | tf_op jit(solution)/shard_map/td,gd->tg/dot_general | solution.py:83
  (2 shorter events, 0.0 us)
Async XLA Ops:
  7.2 1.0 copy-start
  7.2 5.3 %copy-start.8 = (bf16[2048]{0:T(1024)(128)(2,1)S(1)}, bf16[2048]{0:T(1024)(128)(2,1)}, u32[]{:S(2)}) copy-start(bf16[2048]{0:T(1024)(128)(2,1)} %param.16) | copy-start | bytes 12292
  7.2 164.3 %copy-start.4 = (bf16[1,32,2048]{2,1,0:T(8,128)(2,1)S(1)}, bf16[1,32,2048]{2,1,0:T(8,128)(2,1)}, u32[]{:S(2)}) copy-start(bf16[1,32,2048]{2,1,0:T(8,128)(2,1)} %param.17) | copy-start | bytes 393220
  7.2 164.3 %copy-start.7 = (bf16[1,32,2048]{2,1,0:T(8,128)(2,1)S(1)}, bf16[1,32,2048]{2,1,0:T(8,128)(2,1)}, u32[]{:S(2)}) copy-start(bf16[1,32,2048]{2,1,0:T(8,128)(2,1)} %param.13) | copy-start | bytes 393220
  7.2 164.3 %reduce-scatter.2.cloned.1.call-start = ((), (), s32[]{:S(2)}) async-start(), calls=%async_computation.1 | async-start | bytes 4325376 | tf_op jit(solution)/shard_map/reduce_scatter | solution.py:59
  12.4 160.3 %copy-start.6 = (bf16[1,32,2048]{2,1,0:T(8,128)(2,1)S(1)}, bf16[1,32,2048]{2,1,0:T(8,128)(2,1)}, u32[]{:S(2)}) copy-start(bf16[1,32,2048]{2,1,0:T(8,128)(2,1)} %param.18) | copy-start | bytes 393220
  12.4 161.7 %copy-start.1 = (bf16[1,128,2048]{2,1,0:T(8,128)(2,1)S(1)}, bf16[1,128,2048]{2,1,0:T(8,128)(2,1)}, u32[]{:S(2)}) copy-start(bf16[1,128,2048]{2,1,0:T(8,128)(2,1)} %param.14) | copy-start | bytes 1572868
  12.4 162.1 %copy-start.3 = (bf16[1,128,2048]{2,1,0:T(8,128)(2,1)S(1)}, bf16[1,128,2048]{2,1,0:T(8,128)(2,1)}, u32[]{:S(2)}) copy-start(bf16[1,128,2048]{2,1,0:T(8,128)(2,1)} %param.15) | copy-start | bytes 1572868
  12.4 231.2 %all-gather.2.cloned.1.call-start = ((), (), s32[]{:S(2)}) async-start(), calls=%async_computation.2 | async-start | bytes 4325376 | tf_op jit(solution)/shard_map/all_gather | solution.py:78
  172.6 74.5 %copy-start.5 = (bf16[32,2048]{1,0:T(8,128)(2,1)}, bf16[32,2048]{1,0:T(8,128)(2,1)S(1)}, u32[]{:S(2)}) copy-start(bf16[32,2048]{1,0:T(8,128)(2,1)S(1)} %get-tuple-element.62) | copy-start | bytes 393220
  247.3 15.2 %collective-permute-start = (bf16[128,2048]{1,0:T(8,128)(2,1)S(1)}, bf16[128,2048]{1,0:T(8,128)(2,1)}, u32[]{:S(2)}, u32[]{:S(2)}) collective-permute-start(bf16[128,2048]{1,0:T(8,128)(2,1)S(1)} %copy.14), channel_id=1, source_target_pairs={{0,32},{32,0},{64,96},{96,64},{128,160},{160,128},{192,224},{224,1... | collective-permute-start | bytes 1572872 | tf_op jit(solution)/shard_map/cond/branch_0_fun/ppermute | solution.py:32
  250.6 23.2 %collective-permute-start.1 = (bf16[128,2048]{1,0:T(8,128)(2,1)S(1)}, bf16[128,2048]{1,0:T(8,128)(2,1)}, u32[]{:S(2)}, u32[]{:S(2)}) collective-permute-start(bf16[128,2048]{1,0:T(8,128)(2,1)S(1)} %copy.15), channel_id=1, source_target_pairs={{0,32},{32,0},{64,96},{96,64},{128,160},{160,128},{192,224},{224,1... | collective-permute-start | bytes 1572872 | tf_op jit(solution)/shard_map/cond/branch_0_fun/ppermute | solution.py:32
  273.8 9.8 %copy-start.2 = (bf16[1,128,2048]{2,1,0:T(8,128)(2,1)S(1)}, bf16[1,128,2048]{2,1,0:T(8,128)(2,1)}, u32[]{:S(2)}) copy-start(bf16[1,128,2048]{2,1,0:T(8,128)(2,1)} %param.14) | copy-start | bytes 1572868
Sparse Core Ops, SparseCore 0:
  12.5 158.9 reduce-scatter.1
  174.2 69.3 all-gather.1
where the time goes:
time: 295 us
  waiting for transfers between devices  249 us (84%)
  between operations  14.9 us (5%)
  matrix products  11.9 us (4%)
  local copies, waits for them, and re-layouts  9.34 us (3%)
  starting transfers between devices  5.36 us (2%)
  other arithmetic  4.18 us (1%)
    reduce_scatter x1, waiting for transfers between devices, per_device(): lax.psum_scatter((jnp.dot(row_block, weight, preferred_element_type=jnp.f...  159 us
    all_gather x1, waiting for transfers between devices, per_device(): shard_rows = lax.all_gather(dstream, 'tensor', axis=0, tiled=True)  68.8 us
    ppermute x2, waiting for transfers between devices, from_partner(): return lax.ppermute(block, axis, route)  21 us
    unnamed x24, local copies, waits for them, and re-layouts  8.94 us
  transfers between devices with their start and end apart: 4, of which 4 were waited for; matrix products, arithmetic and copies ran while one was open for 0% of the time, Pallas kernels for 0%

commit v1 on v0

v1 whole, which is shorter than its diff:
```python
from functools import partial

import jax
import jax.numpy as jnp
from jax import lax
from jax.experimental import pallas as pl
from jax.experimental.pallas import tpu as pltpu
from jax.sharding import PartitionSpec as P

D = 2048
INNER = 4096
TOK = 1024
GROUP = 128
CHUNKS = 4
WIDE = D // CHUNKS
BF16 = jnp.bfloat16
F32 = jnp.float32
MESH = pl.DeviceIdType.MESH

norm_eps = 1e-05
decay_coef = 0.9
step_span = 1048576.0
inv_width = INNER ** (-0.5)


def plan_rate(step_value):
    phase = step_value.astype(jnp.float32) * (jnp.pi / step_span)
    return 0.02 + 0.04 * (1.0 + jnp.cos(phase))


def flip(digit, mask):
    if mask == 1:
        return digit + 1 - 2 * (digit % 2)
    if mask == 2:
        return (digit + 2) % 4
    return 3 - digit


def cols(k):
    return pl.ds(k * WIDE, WIDE)


def kernel(
    bit,
    attn, resid, weight, velocity, gain, grad_normed, grad_resid, rate,
    stream_out, grad_attn_out, new_weight_out, new_velocity_out,
    acat, wcat, acat_t, s1, r1, keep, s2, r2, s3, r3, full,
    resid_v, gn_v, gr_v, up_v, stream_v, vel_v,
    ga, ga_send, ga_own, g_own, g_send, g_recv, vloc, v_send, v_hop, v_recv, w_hop, w_recv,
    nw_v, nv_v, local_sem, send_sem, recv_sem,
):
    me_r = lax.axis_index("replica")
    me_t = lax.axis_index("tensor")
    y, z, c = me_t // 8, (me_t // 2) % 4, me_t % 2
    relay = bit % 2 == 1

    def at(y_, z_, c_):
        return (me_r, (y_ * 4 + z_) * 2 + c_)

    def peer_at(mask):
        if bit < 2:
            return (me_r - me_r % 4 + flip(me_r % 4, mask), me_t)
        return (flip(me_r // 4, mask) * 4 + me_r % 4, me_t)

    sibling = at(y, z, 1 - c)
    y1, y3 = at(flip(y, 1), z, c), at(flip(y, 3), z, c)
    z_at = [at(y, flip(z, j), c) for j in (1, 2, 3)]
    if relay:
        one, three = peer_at(1)[0], peer_at(3)[0]
        hop1 = (one * (1 - c) + three * c, me_t)
        hop2 = (three * (1 - c) + one * c, me_t)
        peers = [hop1, hop2]
    else:
        hop1 = hop2 = peer_at(1)
        peers = [hop2]

    slots = [0]

    def remote(src, dst, target):
        slot = slots[0]
        slots[0] += 1
        return pltpu.make_async_remote_copy(
            src_ref=src, dst_ref=dst, send_sem=send_sem.at[slot], recv_sem=recv_sem.at[slot],
            device_id=target, device_id_type=MESH,
        )

    local_slots = [0]

    def local(src, dst):
        slot = local_slots[0]
        local_slots[0] += 1
        copy = pltpu.make_async_copy(src, dst, local_sem.at[slot])
        copy.start()
        return copy

    barrier = pltpu.get_barrier_semaphore()
    partners = [sibling, y1, y3] + z_at + peers
    for partner in partners:
        pl.semaphore_signal(barrier, inc=1, device_id=partner, device_id_type=MESH)

    in_a = local(attn.at[:, c], acat.at[:, :, pl.ds(0, GROUP)])
    in_w = local(weight, wcat.at[pl.ds(0, GROUP)])
    in_rest = [
        local(resid, resid_v), local(grad_normed, gn_v),
        local(grad_resid, gr_v), local(velocity, vel_v),
    ]
    pl.semaphore_wait(barrier, len(partners))

    sends = []

    def go(copy):
        copy.start()
        sends.append(copy)
        return copy

    sib_a = go(remote(attn.at[:, 1 - c], acat.at[:, :, pl.ds(GROUP, GROUP)], sibling))
    sib_w = go(remote(weight, wcat.at[pl.ds(GROUP, GROUP)], sibling))
    if relay:
        w_first = go(remote(weight, w_hop, hop1))
        w_last = remote(w_hop, w_recv, hop2)
    else:
        w_last = go(remote(weight, w_recv, hop2))

    in_a.wait()
    in_w.wait()
    sib_a.wait_recv()
    sib_w.wait_recv()

    def rows_for(dest):
        return acat[pl.ds(dest * 4, 4)].reshape(128, 2 * GROUP)

    def product(dest, k):
        return (
            jnp.dot(rows_for(dest), wcat[:, cols(k)], preferred_element_type=F32) * inv_width
        )

    first = [1 if k % 2 == 0 else 3 for k in range(CHUNKS)]
    second = [3 if k % 2 == 0 else 1 for k in range(CHUNKS)]
    along_y = {1: y1, 3: y3}

    step1 = []
    for k in range(CHUNKS):
        s1[k, 0] = product(flip(y, first[k]), k).astype(BF16)
        s1[k, 1] = product(flip(y, 2), k).astype(BF16)
        step1.append(go(remote(s1.at[k], r1.at[k], along_y[first[k]])))
    for k in range(CHUNKS):
        keep[k, 1] = product(flip(y, second[k]), k)
        keep[k, 0] = product(y, k)
    for copy in in_rest:
        copy.wait()
    up_v[...] = gain[...].astype(F32) * gn_v[...].astype(F32)
    acat_t[...] = acat[...].reshape(512, 2 * GROUP).T

    step2 = []
    for k in range(CHUNKS):
        step1[k].wait_recv()
        s2[k] = (keep[k, 1] + r1[k, 1].astype(F32)).astype(BF16)
        step2.append(go(remote(s2.at[k], r2.at[k], along_y[second[k]])))
    step3 = []
    for k in range(CHUNKS):
        step2[k].wait_recv()
        total = keep[k, 0] + r1[k, 0].astype(F32) + r2[k].astype(F32)
        s3[k] = total.astype(BF16).reshape(4, 32, WIDE)
        step3.append([
            go(remote(s3.at[k, flip(z, j)], r3.at[k, j - 1], z_at[j - 1])) for j in (1, 2, 3)
        ])
    squares = jnp.zeros((32, 1), F32)
    inner = jnp.zeros((32, 1), F32)
    for k in range(CHUNKS):
        projected = s3[k, z].astype(F32)
        for j in (1, 2, 3):
            step3[k][j - 1].wait_recv()
            projected += r3[k, j - 1].astype(F32)
        stream = (resid_v[:, cols(k)].astype(F32) + projected).astype(BF16)
        stream_v[:, cols(k)] = stream
        stream32 = stream.astype(F32)
        squares += jnp.sum(stream32 * stream32, axis=-1, keepdims=True)
        inner += jnp.sum(up_v[:, cols(k)] * stream32, axis=-1, keepdims=True)
    out_copies = [local(stream_v, stream_out)]
    inv_rms = lax.rsqrt(squares / D + norm_eps)
    factor = inv_rms * inv_rms * inv_rms * inner / D

    own = y * 4 + z
    gz = []
    for k in range(CHUNKS):
        d = (
            gr_v[:, cols(k)].astype(F32)
            + inv_rms * up_v[:, cols(k)]
            - stream_v[:, cols(k)].astype(F32) * factor
        )
        full[k, own] = d.astype(BF16)
        gz.append([go(remote(full.at[k, own], full.at[k, own], z_at[j - 1])) for j in (1, 2, 3)])
    if relay:
        w_first.wait_recv()
        go(w_last)
    gy = []
    for k in range(CHUNKS):
        for copy in gz[k]:
            copy.wait_recv()
        block = full.at[k, pl.ds(y * 4, 4)]
        gy.append({m: go(remote(block, block, along_y[m])) for m in (1, 3)})
    gf = []
    for k in range(CHUNKS):
        gy[k][first[k]].wait_recv()
        block = full.at[k, pl.ds(flip(y, first[k]) * 4, 4)]
        gf.append(go(remote(block, block, along_y[second[k]])))

    v_first, v_last, g_swap = [], [], []

    def finish_velocity(k):
        g_swap[k].wait_recv()
        grad = ((g_own[k] + g_recv[k].astype(F32)) * inv_width).astype(BF16)
        mine = decay_coef * vel_v[:, cols(k)].astype(F32) + grad.astype(F32)
        vloc[k] = mine
        v_send[k] = mine.astype(BF16)
        if relay:
            v_first.append(go(remote(v_send.at[k], v_hop.at[k], hop1)))
        else:
            v_last.append(go(remote(v_send.at[k], v_recv.at[k], hop2)))

    for k in range(CHUNKS):
        gy[k][second[k]].wait_recv()
        gf[k].wait_recv()
        rows = full[k].reshape(512, WIDE)
        both = jnp.dot(acat_t[...], rows, preferred_element_type=F32)
        g_send[k] = both[GROUP:].astype(BF16)
        g_own[k] = both[:GROUP]
        g_swap.append(go(remote(g_send.at[k], g_recv.at[k], sibling)))
        part = lax.dot_general(
            rows, wcat[:, cols(k)], (((1,), (1,)), ((), ())), preferred_element_type=F32
        )
        ga[...] = part if k == 0 else ga[...] + part
        if k > 0:
            finish_velocity(k - 1)
    finish_velocity(CHUNKS - 1)
    ga_send[...] = (ga[:, GROUP:] * inv_width).astype(BF16).reshape(16, 32, GROUP)
    ga_swap = go(remote(ga_send, grad_attn_out.at[:, c], sibling))
    ga_own[...] = (ga[:, :GROUP] * inv_width).astype(BF16).reshape(16, 32, GROUP)
    out_copies.append(local(ga_own, grad_attn_out.at[:, c]))

    if relay:
        for k in range(CHUNKS):
            v_first[k].wait_recv()
            v_last.append(go(remote(v_hop.at[k], v_recv.at[k], hop2)))
    w_last.wait_recv()
    for k in range(CHUNKS):
        v_last[k].wait_recv()
        mixed = 0.5 * (vloc[k] + v_recv[k].astype(F32))
        nv_v[:, cols(k)] = mixed.astype(BF16)
        mean = 0.5 * (wcat[:GROUP, cols(k)].astype(F32) + w_recv[:, cols(k)].astype(F32))
        nw_v[:, cols(k)] = (mean - rate[0] * mixed).astype(BF16)
        out_copies.append(local(nv_v.at[:, cols(k)], new_velocity_out.at[:, cols(k)]))
        out_copies.append(local(nw_v.at[:, cols(k)], new_weight_out.at[:, cols(k)]))
    ga_swap.wait_recv()
    for copy in out_copies:
        copy.wait()
    for copy in sends:
        copy.wait_send()


def step_with(bit, *operands):
    any_spec = pl.BlockSpec(memory_space=pl.ANY)
    vmem = lambda *shape: pltpu.VMEM(shape, BF16)
    wide = lambda *shape: pltpu.VMEM(shape, F32)
    remote_slots = 2 + 2 + CHUNKS * (1 + 1 + 3 + 3 + 2 + 1 + 1 + 2) + 1
    return pl.pallas_call(
        partial(kernel, bit),
        out_shape=(
            jax.ShapeDtypeStruct((32, D), BF16),
            jax.ShapeDtypeStruct((16, 2, 32, GROUP), BF16),
            jax.ShapeDtypeStruct((GROUP, D), BF16),
            jax.ShapeDtypeStruct((GROUP, D), BF16),
        ),
        in_specs=[any_spec] * 4
        + [pl.BlockSpec(memory_space=pltpu.VMEM)]
        + [any_spec] * 2
        + [pl.BlockSpec(memory_space=pltpu.SMEM)],
        out_specs=(any_spec,) * 4,
        scratch_shapes=[
            vmem(16, 32, 2 * GROUP),
            vmem(2 * GROUP, D),
            vmem(2 * GROUP, 512),
            vmem(CHUNKS, 2, 128, WIDE),
            vmem(CHUNKS, 2, 128, WIDE),
            wide(CHUNKS, 2, 128, WIDE),
            vmem(CHUNKS, 128, WIDE),
            vmem(CHUNKS, 128, WIDE),
            vmem(CHUNKS, 4, 32, WIDE),
            vmem(CHUNKS, 3, 32, WIDE),
            vmem(CHUNKS, 16, 32, WIDE),
            vmem(32, D),
            vmem(32, D),
            vmem(32, D),
            wide(32, D),
            vmem(32, D),
            vmem(GROUP, D),
            wide(512, 2 * GROUP),
            vmem(16, 32, GROUP),
            vmem(16, 32, GROUP),
            wide(CHUNKS, GROUP, WIDE),
            vmem(CHUNKS, GROUP, WIDE),
            vmem(CHUNKS, GROUP, WIDE),
            wide(CHUNKS, GROUP, WIDE),
            vmem(CHUNKS, GROUP, WIDE),
            vmem(CHUNKS, GROUP, WIDE),
            vmem(CHUNKS, GROUP, WIDE),
            vmem(GROUP, D),
            vmem(GROUP, D),
            vmem(GROUP, D),
            vmem(GROUP, D),
            pltpu.SemaphoreType.DMA((6 + 2 + 2 * CHUNKS,)),
            pltpu.SemaphoreType.DMA((remote_slots,)),
            pltpu.SemaphoreType.DMA((remote_slots,)),
        ],
        compiler_params=pltpu.CompilerParams(
            collective_id=bit, has_side_effects=True, vmem_limit_bytes=48 * 1024 * 1024
        ),
        cost_estimate=pl.CostEstimate(
            flops=6 * TOK * GROUP * D, bytes_accessed=8 * 1024 * 1024, transcendentals=64
        ),
        name="step_bit%d" % bit,
    )(*operands)


def per_device(
    attn_out, resid_in, out_weight, velocity, norm_gain, grad_normed, grad_resid, step_count
):
    peer_bit = step_count[0] % 4
    rate = plan_rate(step_count)
    stream, grad_attn, new_weight, new_velocity = lax.switch(
        peer_bit,
        [partial(step_with, bit) for bit in range(4)],
        attn_out.reshape(16, 2, 32, GROUP),
        resid_in[0],
        out_weight[0],
        velocity[0],
        norm_gain.reshape(1, D),
        grad_normed[0],
        grad_resid[0],
        rate,
    )
    return (
        stream[None],
        grad_attn.reshape(1, TOK, GROUP),
        new_weight[None],
        new_velocity[None],
    )


def solution(mesh):
    rows = P("replica", "tensor", None)
    heads = P("replica", None, "tensor")
    return jax.shard_map(
        per_device,
        mesh=mesh,
        in_specs=(heads, rows, rows, rows, P(), rows, rows, P()),
        out_specs=(rows, heads, rows, rows),
        check_vma=False,
    )
```

time: 295 us -> 83.9 us (0.28)
  waiting for transfers between devices: 249 us -> 0 us
  Pallas kernels: 0 us -> 78.3 us
  between operations: 14.9 us -> 1.31 us
  matrix products: 11.9 us -> 0 us
  local copies, waits for them, and re-layouts: 9.34 us -> 3.63 us
  starting transfers between devices: 5.36 us -> 0 us
  other arithmetic: 4.18 us -> 0 us
    reduce_scatter x1 -> x0, waiting for transfers between devices: 159 us -> none  [per_device(): lax.psum_scatter((jnp.dot(row_block, weight, preferred_element_type=jnp.f...]
    pallas_call x0 -> x1, Pallas kernels: none -> 78.3 us  [step_with(): pl.pallas_call(partial(kernel, bit), out_shape=(jax.ShapeDtypeStruct((32,...]
    all_gather x1 -> x0, waiting for transfers between devices: 68.8 us -> none  [per_device(): shard_rows = lax.all_gather(dstream, 'tensor', axis=0, tiled=True)]
    ppermute x2 -> x0, waiting for transfers between devices: 21 us -> none  [from_partner(): return lax.ppermute(block, axis, route)]
    dot_general x3 -> x0, matrix products: 11.9 us -> none  [the longest x1 4.24 us: per_device(): jnp.dot(row_block, weight, preferred_element_type=jnp.float32) * inv_width]
    unnamed x24 -> x6, local copies, waits for them, and re-layouts: 8.94 us -> 3.62 us
    ppermute x2 -> x0, starting transfers between devices: 5.28 us -> none  [from_partner(): return lax.ppermute(block, axis, route)]
  transfers between devices with their start and end apart: 4 -> 0, of which waited for: 4 -> 0; matrix products, arithmetic and copies ran while one was open for 0% -> 0% of each run, Pallas kernels for 0% -> 0%
where the time goes in v1:
time: 83.9 us; the launch traced here: 83.6 us
  Pallas kernels  78.3 us (93%)
  local copies, waits for them, and re-layouts  3.63 us (4%)
  between operations  1.31 us (2%)
    pallas_call x1, Pallas kernels, step_with(): pl.pallas_call(partial(kernel, bit), out_shape=(jax.ShapeDtypeStruct((32,...  78.3 us
    unnamed x6, local copies, waits for them, and re-layouts  3.62 us

profile of v1, /device:TPU:1, one launch (start us, length us, event | category | flops | bytes accessed | tf_op | source)
XLA Modules:
  0.0 83.6 jit_solution(9714425678894523013)
XLA Ops:
  1.3 0.0 copy-start
  1.3 0.7 copy-done
  2.0 78.7 %conditional.1 = ((bf16[32,2048]{1,0:T(8,128)(2,1)S(1)}, bf16[16,2,32,128]{3,2,1,0:T(8,128)(2,1)S(1)}, bf16[128,2048]{1,0:T(8,128)(2,1)S(1)}, bf16[128,2048]{1,0:T(8,128)(2,1)S(1)})) conditional(s32[]{:T(128)} %clamp.3, (bf16[1,1024,128]{2,1,0:T(8,128)(2,1)}, bf16[1,32,2048]{2,1,0:T(8,128)(2,1)}, ...), branch_computations={%region_0.1_spmd, %region_1.2_spmd, %region_2.3_spmd, %region_3.4_... | conditional | flops 1610612736 | bytes 8396864 | solution.py:330
  2.1 78.3 %step_bit0.2 = (bf16[32,2048]{1,0:T(8,128)(2,1)S(1)}, bf16[16,2,32,128]{3,2,1,0:T(8,128)(2,1)S(1)}, bf16[128,2048]{1,0:T(8,128)(2,1)S(1)}, bf16[128,2048]{1,0:T(8,128)(2,1)S(1)}) custom-call(bf16[16,2,32,128]{3,2,1,0:T(8,128)(2,1)} %bitcast.44, bf16[32,2048]{1,0:T(8,128)(2,1)} %bitcast.48, bf16[128,2048]{1,0:T(8,128)(2,1)} %bitcast.36, ...), custom_call_target="tpu_custom_call" | custom-call | flops 1610612736 | bytes 8388608 | tf_op jit(solution)/shard_map/cond/branch_0_fun/step_bit0/pallas_call | solution.py:266
  80.6 0.7 copy.33
  81.3 0.7 copy.34
  82.0 0.8 copy.35
  82.8 0.8 copy.36
  (1 shorter events, 0.0 us)
Async XLA Ops:
  1.3 0.7 copy-start

commit v2 on v1

--- a/solution.py
+++ b/solution.py
@@ -13,6 +13,12 @@
 GROUP = 128
 CHUNKS = 4
 WIDE = D // CHUNKS
+AHEAD = CHUNKS // 2
+QUARTER = CHUNKS // 4
+PIECES = 8
+ONLY = ((0,) * 8, (0, 1, 2, 3, 4, 5, 6, 7))
+FIRST = ((0,) * 8, (0, 0, 2, 2, 4, 4, 6, 6))
+LAST = ((3,) * 8, (8,) * 8)
 BF16 = jnp.bfloat16
 F32 = jnp.float32
 MESH = pl.DeviceIdType.MESH
@@ -45,7 +51,7 @@
     attn, resid, weight, velocity, gain, grad_normed, grad_resid, rate,
     stream_out, grad_attn_out, new_weight_out, new_velocity_out,
     acat, wcat, acat_t, s1, r1, keep, s2, r2, s3, r3, full,
-    resid_v, gn_v, gr_v, up_v, stream_v, vel_v,
+    resid_v, gain_v, gn_v, gr_v, up_v, stream_v, vel_v,
     ga, ga_send, ga_own, g_own, g_send, g_recv, vloc, v_send, v_hop, v_recv, w_hop, w_recv,
     nw_v, nv_v, local_sem, send_sem, recv_sem,
 ):
@@ -101,7 +107,7 @@
     in_a = local(attn.at[:, c], acat.at[:, :, pl.ds(0, GROUP)])
     in_w = local(weight, wcat.at[pl.ds(0, GROUP)])
     in_rest = [
-        local(resid, resid_v), local(grad_normed, gn_v),
+        local(resid, resid_v), local(gain, gain_v), local(grad_normed, gn_v),
         local(grad_resid, gr_v), local(velocity, vel_v),
     ]
     pl.semaphore_wait(barrier, len(partners))
@@ -115,12 +121,28 @@
 
     sib_a = go(remote(attn.at[:, 1 - c], acat.at[:, :, pl.ds(GROUP, GROUP)], sibling))
     sib_w = go(remote(weight, wcat.at[pl.ds(GROUP, GROUP)], sibling))
-    if relay:
-        w_first = go(remote(weight, w_hop, hop1))
-        w_last = remote(w_hop, w_recv, hop2)
-    else:
-        w_last = go(remote(weight, w_recv, hop2))
-
+    piece = GROUP // PIECES
+    rows = [pl.ds(i * piece, piece) for i in range(PIECES)]
+    w_first = [remote(weight.at[r], w_hop.at[r], hop1) for r in rows] if relay else []
+    w_last = [
+        remote((w_hop if relay else weight).at[r], w_recv.at[r], hop2) for r in rows
+    ]
+    sends.extend(w_first + w_last)
+
+    def point(i):
+        if relay:
+            for n in range(PIECES):
+                if i == FIRST[bit // 2][n]:
+                    w_first[n].start()
+                if i == LAST[bit // 2][n]:
+                    w_first[n].wait_recv()
+                    w_last[n].start()
+        else:
+            for n in range(PIECES):
+                if i == ONLY[bit // 2][n]:
+                    w_last[n].start()
+
+    point(0)
     in_a.wait()
     in_w.wait()
     sib_a.wait_recv()
@@ -129,44 +151,49 @@
     def rows_for(dest):
         return acat[pl.ds(dest * 4, 4)].reshape(128, 2 * GROUP)
 
-    def product(dest, k):
+    along_y = {1: y1, 3: y3}
+    first, second = (1, 3), (3, 1)
+    half = WIDE // 2
+
+    def part(k, h):
+        return pl.ds(k * WIDE + h * half, half)
+
+    def product(dest, k, h):
         return (
-            jnp.dot(rows_for(dest), wcat[:, cols(k)], preferred_element_type=F32) * inv_width
+            jnp.dot(rows_for(dest), wcat[:, part(k, h)], preferred_element_type=F32) * inv_width
         )
 
-    first = [1 if k % 2 == 0 else 3 for k in range(CHUNKS)]
-    second = [3 if k % 2 == 0 else 1 for k in range(CHUNKS)]
-    along_y = {1: y1, 3: y3}
-
-    step1 = []
-    for k in range(CHUNKS):
-        s1[k, 0] = product(flip(y, first[k]), k).astype(BF16)
-        s1[k, 1] = product(flip(y, 2), k).astype(BF16)
-        step1.append(go(remote(s1.at[k], r1.at[k], along_y[first[k]])))
-    for k in range(CHUNKS):
-        keep[k, 1] = product(flip(y, second[k]), k)
-        keep[k, 0] = product(y, k)
-    for copy in in_rest:
-        copy.wait()
-    up_v[...] = gain[...].astype(F32) * gn_v[...].astype(F32)
-    acat_t[...] = acat[...].reshape(512, 2 * GROUP).T
-
-    step2 = []
-    for k in range(CHUNKS):
-        step1[k].wait_recv()
-        s2[k] = (keep[k, 1] + r1[k, 1].astype(F32)).astype(BF16)
-        step2.append(go(remote(s2.at[k], r2.at[k], along_y[second[k]])))
-    step3 = []
-    for k in range(CHUNKS):
-        step2[k].wait_recv()
-        total = keep[k, 0] + r1[k, 0].astype(F32) + r2[k].astype(F32)
-        s3[k] = total.astype(BF16).reshape(4, 32, WIDE)
-        step3.append([
+    step1, step2, step3 = {}, {}, {}
+
+    def send1(k):
+        for h in (0, 1):
+            s1[k, h, 0] = product(flip(y, first[h]), k, h).astype(BF16)
+            s1[k, h, 1] = product(flip(y, 2), k, h).astype(BF16)
+            step1[k, h] = go(remote(s1.at[k, h], r1.at[k, h], along_y[first[h]]))
+
+    def hold(k):
+        for h in (0, 1):
+            keep[k, h, 1] = product(flip(y, second[h]), k, h)
+            keep[k, h, 0] = product(y, k, h)
+
+    def send2(k):
+        for h in (0, 1):
+            step1[k, h].wait_recv()
+            s2[k, h] = (keep[k, h, 1] + r1[k, h, 1].astype(F32)).astype(BF16)
+            step2[k, h] = go(remote(s2.at[k, h], r2.at[k, h], along_y[second[h]]))
+
+    def send3(k):
+        for h in (0, 1):
+            step2[k, h].wait_recv()
+            total = keep[k, h, 0] + r1[k, h, 0].astype(F32) + r2[k, h].astype(F32)
+            s3[k, :, :, pl.ds(h * half, half)] = total.astype(BF16).reshape(4, 32, half)
+        step3[k] = [
             go(remote(s3.at[k, flip(z, j)], r3.at[k, j - 1], z_at[j - 1])) for j in (1, 2, 3)
-        ])
-    squares = jnp.zeros((32, 1), F32)
-    inner = jnp.zeros((32, 1), F32)
-    for k in range(CHUNKS):
+        ]
+
+    sums = [jnp.zeros((32, 1), F32), jnp.zeros((32, 1), F32)]
+
+    def add_stream(k):
         projected = s3[k, z].astype(F32)
         for j in (1, 2, 3):
             step3[k][j - 1].wait_recv()
@@ -174,75 +201,137 @@
         stream = (resid_v[:, cols(k)].astype(F32) + projected).astype(BF16)
         stream_v[:, cols(k)] = stream
         stream32 = stream.astype(F32)
-        squares += jnp.sum(stream32 * stream32, axis=-1, keepdims=True)
-        inner += jnp.sum(up_v[:, cols(k)] * stream32, axis=-1, keepdims=True)
-    out_copies = [local(stream_v, stream_out)]
+        sums[0] += jnp.sum(stream32 * stream32, axis=-1, keepdims=True)
+        sums[1] += jnp.sum(up_v[:, cols(k)] * stream32, axis=-1, keepdims=True)
+
+    for k in range(AHEAD):
+        send1(k)
+    for k in range(AHEAD):
+        hold(k)
+    for k in range(CHUNKS):
+        send2(k)
+        if k >= 1:
+            send3(k - 1)
+        if k + AHEAD < CHUNKS:
+            send1(k + AHEAD)
+            hold(k + AHEAD)
+        if k == 1:
+            for copy in in_rest:
+                copy.wait()
+            gain32 = gain_v[...].astype(F32)
+            for i in range(D // 128):
+                lanes = pl.ds(i * 128, 128)
+                up_v[:, lanes] = gain32[i : i + 1] * gn_v[:, lanes].astype(F32)
+            acat_t[...] = acat[...].reshape(512, 2 * GROUP).T
+        if k >= 2:
+            add_stream(k - 2)
+        if (k + 1) % QUARTER == 0:
+            point((k + 1) // QUARTER)
+    send3(CHUNKS - 1)
+    add_stream(CHUNKS - 2)
+    add_stream(CHUNKS - 1)
+    squares, inner = sums
     inv_rms = lax.rsqrt(squares / D + norm_eps)
     factor = inv_rms * inv_rms * inv_rms * inner / D
 
     own = y * 4 + z
-    gz = []
-    for k in range(CHUNKS):
+    gz, gy, gf = {}, {}, {}
+
+    def dstream(k):
         d = (
             gr_v[:, cols(k)].astype(F32)
             + inv_rms * up_v[:, cols(k)]
             - stream_v[:, cols(k)].astype(F32) * factor
         )
         full[k, own] = d.astype(BF16)
-        gz.append([go(remote(full.at[k, own], full.at[k, own], z_at[j - 1])) for j in (1, 2, 3)])
-    if relay:
-        w_first.wait_recv()
-        go(w_last)
-    gy = []
-    for k in range(CHUNKS):
-        for copy in gz[k]:
-            copy.wait_recv()
-        block = full.at[k, pl.ds(y * 4, 4)]
-        gy.append({m: go(remote(block, block, along_y[m])) for m in (1, 3)})
-    gf = []
-    for k in range(CHUNKS):
-        gy[k][first[k]].wait_recv()
-        block = full.at[k, pl.ds(flip(y, first[k]) * 4, 4)]
-        gf.append(go(remote(block, block, along_y[second[k]])))
-
-    v_first, v_last, g_swap = [], [], []
-
-    def finish_velocity(k):
+
+    def gather_own(k):
+        block = full.at[k, own]
+        gy[k] = {m: [go(remote(block, block, along_y[m]))] for m in (1, 3)}
+
+    def gather_z(k):
+        block = full.at[k, own]
+        gz[k] = [go(remote(block, block, z_at[j - 1])) for j in (1, 2, 3)]
+
+    def gather_y(k):
+        for j in (1, 2, 3):
+            gz[k][j - 1].wait_recv()
+            block = full.at[k, y * 4 + flip(z, j)]
+            for m in (1, 3):
+                gy[k][m].append(go(remote(block, block, along_y[m])))
+
+    def forward_y(k):
+        for h in (0, 1):
+            for copy in gy[k][first[h]]:
+                copy.wait_recv()
+            block = full.at[k, pl.ds(flip(y, first[h]) * 4, 4), :, pl.ds(h * half, half)]
+            gf[k, h] = go(remote(block, block, along_y[second[h]]))
+
+    v_first, v_last, g_swap = {}, {}, {}
+
+    def weight_part(k):
+        gf[k, 0].wait_recv()
+        gf[k, 1].wait_recv()
+        rows = full[k].reshape(512, WIDE)
+        both = jnp.dot(acat_t[...], rows, preferred_element_type=F32)
+        g_send[k] = both[GROUP:].astype(BF16)
+        g_own[k] = both[:GROUP]
+        g_swap[k] = go(remote(g_send.at[k], g_recv.at[k], sibling))
+
+    def attn_part(k):
+        rows = full[k].reshape(512, WIDE)
+        share = lax.dot_general(
+            rows, wcat[:, cols(k)], (((1,), (1,)), ((), ())), preferred_element_type=F32
+        )
+        ga[...] = share if k == 0 else ga[...] + share
+
+    def send_velocity(k):
         g_swap[k].wait_recv()
         grad = ((g_own[k] + g_recv[k].astype(F32)) * inv_width).astype(BF16)
         mine = decay_coef * vel_v[:, cols(k)].astype(F32) + grad.astype(F32)
         vloc[k] = mine
         v_send[k] = mine.astype(BF16)
         if relay:
-            v_first.append(go(remote(v_send.at[k], v_hop.at[k], hop1)))
+            v_first[k] = go(remote(v_send.at[k], v_hop.at[k], hop1))
         else:
-            v_last.append(go(remote(v_send.at[k], v_recv.at[k], hop2)))
+            v_last[k] = go(remote(v_send.at[k], v_recv.at[k], hop2))
+
+    def relay_velocity(k):
+        if relay:
+            v_first[k].wait_recv()
+            v_last[k] = go(remote(v_hop.at[k], v_recv.at[k], hop2))
 
     for k in range(CHUNKS):
-        gy[k][second[k]].wait_recv()
-        gf[k].wait_recv()
-        rows = full[k].reshape(512, WIDE)
-        both = jnp.dot(acat_t[...], rows, preferred_element_type=F32)
-        g_send[k] = both[GROUP:].astype(BF16)
-        g_own[k] = both[:GROUP]
-        g_swap.append(go(remote(g_send.at[k], g_recv.at[k], sibling)))
-        part = lax.dot_general(
-            rows, wcat[:, cols(k)], (((1,), (1,)), ((), ())), preferred_element_type=F32
-        )
-        ga[...] = part if k == 0 else ga[...] + part
-        if k > 0:
-            finish_velocity(k - 1)
-    finish_velocity(CHUNKS - 1)
+        dstream(k)
+        gather_own(k)
+        if k < AHEAD:
+            gather_z(k)
+    out_copies = [local(stream_v, stream_out)]
+    for i in range(CHUNKS + 3):
+        if i < CHUNKS:
+            gather_y(i)
+            if i + AHEAD < CHUNKS:
+                gather_z(i + AHEAD)
+            if (i + 1) % QUARTER == 0:
+                point(4 + (i + 1) // QUARTER)
+        if 0 <= i - 1 < CHUNKS:
+            forward_y(i - 1)
+        if 0 <= i - 3:
+            send_velocity(i - 3)
+            if i - 4 >= 0 and bit == 1:
+                relay_velocity(i - 4)
+        if 0 <= i - 2 < CHUNKS:
+            weight_part(i - 2)
+            attn_part(i - 2)
     ga_send[...] = (ga[:, GROUP:] * inv_width).astype(BF16).reshape(16, 32, GROUP)
     ga_swap = go(remote(ga_send, grad_attn_out.at[:, c], sibling))
     ga_own[...] = (ga[:, :GROUP] * inv_width).astype(BF16).reshape(16, 32, GROUP)
     out_copies.append(local(ga_own, grad_attn_out.at[:, c]))
-
-    if relay:
-        for k in range(CHUNKS):
-            v_first[k].wait_recv()
-            v_last.append(go(remote(v_hop.at[k], v_recv.at[k], hop2)))
-    w_last.wait_recv()
+    for k in range(CHUNKS - 1 if bit == 1 else 0, CHUNKS):
+        relay_velocity(k)
+
+    for copy in w_last:
+        copy.wait_recv()
     for k in range(CHUNKS):
         v_last[k].wait_recv()
         mixed = 0.5 * (vloc[k] + v_recv[k].astype(F32))
@@ -262,7 +351,7 @@
     any_spec = pl.BlockSpec(memory_space=pl.ANY)
     vmem = lambda *shape: pltpu.VMEM(shape, BF16)
     wide = lambda *shape: pltpu.VMEM(shape, F32)
-    remote_slots = 2 + 2 + CHUNKS * (1 + 1 + 3 + 3 + 2 + 1 + 1 + 2) + 1
+    remote_slots = 2 + 2 + CHUNKS * (2 + 2 + 3 + 3 + 8 + 2 + 1 + 2) + 1 + 2 * PIECES
     return pl.pallas_call(
         partial(kernel, bit),
         out_shape=(
@@ -271,24 +360,22 @@
             jax.ShapeDtypeStruct((GROUP, D), BF16),
             jax.ShapeDtypeStruct((GROUP, D), BF16),
         ),
-        in_specs=[any_spec] * 4
-        + [pl.BlockSpec(memory_space=pltpu.VMEM)]
-        + [any_spec] * 2
-        + [pl.BlockSpec(memory_space=pltpu.SMEM)],
+        in_specs=[any_spec] * 7 + [pl.BlockSpec(memory_space=pltpu.SMEM)],
         out_specs=(any_spec,) * 4,
         scratch_shapes=[
             vmem(16, 32, 2 * GROUP),
             vmem(2 * GROUP, D),
             vmem(2 * GROUP, 512),
-            vmem(CHUNKS, 2, 128, WIDE),
-            vmem(CHUNKS, 2, 128, WIDE),
-            wide(CHUNKS, 2, 128, WIDE),
-            vmem(CHUNKS, 128, WIDE),
-            vmem(CHUNKS, 128, WIDE),
+            vmem(CHUNKS, 2, 2, 128, WIDE // 2),
+            vmem(CHUNKS, 2, 2, 128, WIDE // 2),
+            wide(CHUNKS, 2, 2, 128, WIDE // 2),
+            vmem(CHUNKS, 2, 128, WIDE // 2),
+            vmem(CHUNKS, 2, 128, WIDE // 2),
             vmem(CHUNKS, 4, 32, WIDE),
             vmem(CHUNKS, 3, 32, WIDE),
             vmem(CHUNKS, 16, 32, WIDE),
             vmem(32, D),
+            vmem(16, 128),
             vmem(32, D),
             vmem(32, D),
             wide(32, D),
@@ -308,7 +395,7 @@
             vmem(GROUP, D),
             vmem(GROUP, D),
             vmem(GROUP, D),
-            pltpu.SemaphoreType.DMA((6 + 2 + 2 * CHUNKS,)),
+            pltpu.SemaphoreType.DMA((7 + 2 + 2 * CHUNKS,)),
             pltpu.SemaphoreType.DMA((remote_slots,)),
             pltpu.SemaphoreType.DMA((remote_slots,)),
         ],
@@ -334,7 +421,7 @@
         resid_in[0],
         out_weight[0],
         velocity[0],
-        norm_gain.reshape(1, D),
+        norm_gain.reshape(16, 128),
         grad_normed[0],
         grad_resid[0],
         rate,

time: 83.9 us -> 129 us (1.54)
  Pallas kernels: 78.3 us -> 123 us
    pallas_call x1, Pallas kernels: 78.3 us -> 123 us  [step_with(): pl.pallas_call(partial(kernel, bit), out_shape=(jax.ShapeDtypeStruct((32,...]
where the time goes in v2:
time: 129 us
  Pallas kernels  123 us (95%)
  local copies, waits for them, and re-layouts  3.62 us (3%)
  between operations  1.31 us (1%)
    pallas_call x1, Pallas kernels, step_with(): pl.pallas_call(partial(kernel, bit), out_shape=(jax.ShapeDtypeStruct((32,...  123 us
    unnamed x6, local copies, waits for them, and re-layouts  3.62 us

profile of v2, /device:TPU:1, one launch (start us, length us, event | category | flops | bytes accessed | tf_op | source)
XLA Modules:
  0.0 128.7 jit_solution(1188214978562062404)
XLA Ops:
  1.3 0.0 copy-start
  1.3 0.7 copy-done
  2.0 123.8 %conditional.1 = ((bf16[32,2048]{1,0:T(8,128)(2,1)S(1)}, bf16[16,2,32,128]{3,2,1,0:T(8,128)(2,1)S(1)}, bf16[128,2048]{1,0:T(8,128)(2,1)S(1)}, bf16[128,2048]{1,0:T(8,128)(2,1)S(1)})) conditional(s32[]{:T(128)} %clamp.3, (bf16[1,1024,128]{2,1,0:T(8,128)(2,1)}, bf16[1,32,2048]{2,1,0:T(8,128)(2,1)}, ...), branch_computations={%region_0.1_spmd, %region_1.2_spmd, %region_2.3_spmd, %region_3.4_... | conditional | flops 1610612736 | bytes 8388672 | solution.py:417
  2.1 123.5 %step_bit2.2 = (bf16[32,2048]{1,0:T(8,128)(2,1)S(1)}, bf16[16,2,32,128]{3,2,1,0:T(8,128)(2,1)S(1)}, bf16[128,2048]{1,0:T(8,128)(2,1)S(1)}, bf16[128,2048]{1,0:T(8,128)(2,1)S(1)}) custom-call(bf16[16,2,32,128]{3,2,1,0:T(8,128)(2,1)} %bitcast.50, bf16[32,2048]{1,0:T(8,128)(2,1)} %bitcast.54, bf16[128,2048]{1,0:T(8,128)(2,1)} %bitcast.42, ...), custom_call_target="tpu_custom_call" | custom-call | flops 1610612736 | bytes 8388608 | tf_op jit(solution)/shard_map/cond/branch_2_fun/step_bit2/pallas_call | solution.py:355
  125.8 0.7 copy.33
  126.4 0.7 copy.34
  127.1 0.8 copy.35
  127.9 0.8 copy.36
Async XLA Ops:
  1.3 0.7 copy-start

commit v3 on v2

--- a/solution.py
+++ b/solution.py
@@ -16,9 +16,9 @@
 AHEAD = CHUNKS // 2
 QUARTER = CHUNKS // 4
 PIECES = 8
-ONLY = ((0,) * 8, (0, 1, 2, 3, 4, 5, 6, 7))
-FIRST = ((0,) * 8, (0, 0, 2, 2, 4, 4, 6, 6))
-LAST = ((3,) * 8, (8,) * 8)
+ONLY = ((0,) * 8, (0, 0, 1, 1, 2, 3, 5, 7))
+FIRST = ((0,) * 8, (0, 0, 1, 1, 2, 2, 3, 3))
+LAST = ((3,) * 8, (7, 7, 8, 8, 8, 8, 8, 8))
 BF16 = jnp.bfloat16
 F32 = jnp.float32
 MESH = pl.DeviceIdType.MESH
@@ -50,7 +50,7 @@
     bit,
     attn, resid, weight, velocity, gain, grad_normed, grad_resid, rate,
     stream_out, grad_attn_out, new_weight_out, new_velocity_out,
-    acat, wcat, acat_t, s1, r1, keep, s2, r2, s3, r3, full,
+    acat, wcat, acat_t, pcat, wp, keep, s2, r2, s3, r3, full,
     resid_v, gain_v, gn_v, gr_v, up_v, stream_v, vel_v,
     ga, ga_send, ga_own, g_own, g_send, g_recv, vloc, v_send, v_hop, v_recv, w_hop, w_recv,
     nw_v, nv_v, local_sem, send_sem, recv_sem,
@@ -100,7 +100,8 @@
         return copy
 
     barrier = pltpu.get_barrier_semaphore()
-    partners = [sibling, y1, y3] + z_at + peers
+    across = {1: at(flip(y, 1), z, 1 - c), 3: at(flip(y, 3), z, 1 - c)}
+    partners = [sibling, y1, y3, across[1], across[3]] + z_at + peers
     for partner in partners:
         pl.semaphore_signal(barrier, inc=1, device_id=partner, device_id_type=MESH)
 
@@ -119,10 +120,40 @@
         sends.append(copy)
         return copy
 
+    along_y = {1: y1, 3: y3}
+    first, second = (1, 3), (3, 1)
+    half = WIDE // 2
+
+    def part(k, h):
+        return pl.ds(k * WIDE + h * half, half)
+
+    own_lanes, other_lanes = pl.ds(0, GROUP), pl.ds(GROUP, GROUP)
+    attn_y, weight_y, weight_over = {}, {}, {}
+
+    def send_attn(h):
+        attn_y[h] = []
+        for slot, mask in enumerate((first[h], 2)):
+            dest = pl.ds(flip(y, mask) * 4, 4)
+            for core, lanes, target in (
+                (c, own_lanes, along_y[first[h]]), (1 - c, other_lanes, across[first[h]])
+            ):
+                there = pcat.at[h, slot, :, :, lanes]
+                attn_y[h].append(go(remote(attn.at[dest, core], there, target)))
+
+    def send_weight(k):
+        for h in (0, 1):
+            there = wp.at[k, h, own_lanes]
+            weight_y[k, h] = go(remote(weight.at[:, part(k, h)], there, along_y[first[h]]))
+
+    send_attn(0)
+    send_attn(1)
+    send_weight(0)
     sib_a = go(remote(attn.at[:, 1 - c], acat.at[:, :, pl.ds(GROUP, GROUP)], sibling))
     sib_w = go(remote(weight, wcat.at[pl.ds(GROUP, GROUP)], sibling))
     piece = GROUP // PIECES
     rows = [pl.ds(i * piece, piece) for i in range(PIECES)]
+    for k in range(1, AHEAD):
+        send_weight(k)
     w_first = [remote(weight.at[r], w_hop.at[r], hop1) for r in rows] if relay else []
     w_last = [
         remote((w_hop if relay else weight).at[r], w_recv.at[r], hop2) for r in rows
@@ -151,41 +182,41 @@
     def rows_for(dest):
         return acat[pl.ds(dest * 4, 4)].reshape(128, 2 * GROUP)
 
-    along_y = {1: y1, 3: y3}
-    first, second = (1, 3), (3, 1)
-    half = WIDE // 2
-
-    def part(k, h):
-        return pl.ds(k * WIDE + h * half, half)
-
     def product(dest, k, h):
         return (
             jnp.dot(rows_for(dest), wcat[:, part(k, h)], preferred_element_type=F32) * inv_width
         )
 
-    step1, step2, step3 = {}, {}, {}
-
-    def send1(k):
-        for h in (0, 1):
-            s1[k, h, 0] = product(flip(y, first[h]), k, h).astype(BF16)
-            s1[k, h, 1] = product(flip(y, 2), k, h).astype(BF16)
-            step1[k, h] = go(remote(s1.at[k, h], r1.at[k, h], along_y[first[h]]))
+    step2, step3 = {}, {}
 
     def hold(k):
         for h in (0, 1):
             keep[k, h, 1] = product(flip(y, second[h]), k, h)
             keep[k, h, 0] = product(y, k, h)
 
+    def fetch(k):
+        for h in (0, 1):
+            weight_y[k, h].wait_recv()
+            here, there = wp.at[k, h, own_lanes], wp.at[k, h, other_lanes]
+            weight_over[k, h] = go(remote(here, there, sibling))
+
     def send2(k):
         for h in (0, 1):
-            step1[k, h].wait_recv()
-            s2[k, h] = (keep[k, h, 1] + r1[k, h, 1].astype(F32)).astype(BF16)
+            if k == 0:
+                for copy in attn_y[h]:
+                    copy.wait_recv()
+            weight_over[k, h].wait_recv()
+            more = jnp.dot(
+                pcat[h].reshape(256, 2 * GROUP), wp[k, h], preferred_element_type=F32
+            ) * inv_width
+            s2[k, h] = (keep[k, h, 1] + more[128:]).astype(BF16)
             step2[k, h] = go(remote(s2.at[k, h], r2.at[k, h], along_y[second[h]]))
+            keep[k, h, 0] += more[:128]
 
     def send3(k):
         for h in (0, 1):
             step2[k, h].wait_recv()
-            total = keep[k, h, 0] + r1[k, h, 0].astype(F32) + r2[k, h].astype(F32)
+            total = keep[k, h, 0] + r2[k, h].astype(F32)
             s3[k, :, :, pl.ds(h * half, half)] = total.astype(BF16).reshape(4, 32, half)
         step3[k] = [
             go(remote(s3.at[k, flip(z, j)], r3.at[k, j - 1], z_at[j - 1])) for j in (1, 2, 3)
@@ -204,17 +235,19 @@
         sums[0] += jnp.sum(stream32 * stream32, axis=-1, keepdims=True)
         sums[1] += jnp.sum(up_v[:, cols(k)] * stream32, axis=-1, keepdims=True)
 
-    for k in range(AHEAD):
-        send1(k)
-    for k in range(AHEAD):
-        hold(k)
+    hold(0)
+    hold(1)
+    fetch(0)
     for k in range(CHUNKS):
+        if k + AHEAD < CHUNKS:
+            send_weight(k + AHEAD)
+        if k + 1 < CHUNKS:
+            fetch(k + 1)
         send2(k)
+        if k + 2 < CHUNKS:
+            hold(k + 2)
         if k >= 1:
             send3(k - 1)
-        if k + AHEAD < CHUNKS:
-            send1(k + AHEAD)
-            hold(k + AHEAD)
         if k == 1:
             for copy in in_rest:
                 copy.wait()
@@ -351,7 +384,7 @@
     any_spec = pl.BlockSpec(memory_space=pl.ANY)
     vmem = lambda *shape: pltpu.VMEM(shape, BF16)
     wide = lambda *shape: pltpu.VMEM(shape, F32)
-    remote_slots = 2 + 2 + CHUNKS * (2 + 2 + 3 + 3 + 8 + 2 + 1 + 2) + 1 + 2 * PIECES
+    remote_slots = 2 + 2 + CHUNKS * (2 + 2 + 2 + 3 + 3 + 8 + 2 + 1 + 2) + 9 + 2 * PIECES
     return pl.pallas_call(
         partial(kernel, bit),
         out_shape=(
@@ -366,8 +399,8 @@
             vmem(16, 32, 2 * GROUP),
             vmem(2 * GROUP, D),
             vmem(2 * GROUP, 512),
-            vmem(CHUNKS, 2, 2, 128, WIDE // 2),
-            vmem(CHUNKS, 2, 2, 128, WIDE // 2),
+            vmem(2, 2, 4, 32, 2 * GROUP),
+            vmem(CHUNKS, 2, 2 * GROUP, WIDE // 2),
             wide(CHUNKS, 2, 2, 128, WIDE // 2),
             vmem(CHUNKS, 2, 128, WIDE // 2),
             vmem(CHUNKS, 2, 128, WIDE // 2),

time: 129 us -> 146 us (1.13)
  the two profiles are of different devices: /device:TPU:1 before, /device:TPU:2 now
where the time goes in v3:
time: 146 us; the launch traced here: 145 us
  Pallas kernels  140 us (96%)
  local copies, waits for them, and re-layouts  3.62 us (2%)
    pallas_call x1, Pallas kernels, step_with(): pl.pallas_call(partial(kernel, bit), out_shape=(jax.ShapeDtypeStruct((32,...  140 us
    unnamed x6, local copies, waits for them, and re-layouts  3.62 us

profile of v3, /device:TPU:2, one launch (start us, length us, event | category | flops | bytes accessed | tf_op | source)
XLA Modules:
  0.0 145.5 jit_solution(17797738590128962513)
XLA Ops:
  1.3 0.0 copy-start
  1.3 0.7 copy-done
  2.0 140.6 %conditional.1 = ((bf16[32,2048]{1,0:T(8,128)(2,1)S(1)}, bf16[16,2,32,128]{3,2,1,0:T(8,128)(2,1)S(1)}, bf16[128,2048]{1,0:T(8,128)(2,1)S(1)}, bf16[128,2048]{1,0:T(8,128)(2,1)S(1)})) conditional(s32[]{:T(128)} %clamp.3, (bf16[1,1024,128]{2,1,0:T(8,128)(2,1)}, bf16[1,32,2048]{2,1,0:T(8,128)(2,1)}, ...), branch_computations={%region_0.1_spmd, %region_1.2_spmd, %region_2.3_spmd, %region_3.4_... | conditional | flops 1610612736 | bytes 8388672 | solution.py:450
  2.1 140.3 %step_bit3.2 = (bf16[32,2048]{1,0:T(8,128)(2,1)S(1)}, bf16[16,2,32,128]{3,2,1,0:T(8,128)(2,1)S(1)}, bf16[128,2048]{1,0:T(8,128)(2,1)S(1)}, bf16[128,2048]{1,0:T(8,128)(2,1)S(1)}) custom-call(bf16[16,2,32,128]{3,2,1,0:T(8,128)(2,1)} %bitcast.51, bf16[32,2048]{1,0:T(8,128)(2,1)} %bitcast.55, bf16[128,2048]{1,0:T(8,128)(2,1)} %bitcast.43, ...), custom_call_target="tpu_custom_call" | custom-call | flops 1610612736 | bytes 8388608 | tf_op jit(solution)/shard_map/cond/branch_3_fun/step_bit3/pallas_call | solution.py:388
  142.5 0.7 copy.33
  143.2 0.7 copy.34
  143.9 0.8 copy.35
  144.7 0.8 copy.36
Async XLA Ops:
  1.3 0.7 copy-start
